TPU v7x, 32 devices: a whole 2x2x4 slice. The times are simulated.
32 devices in a mesh: groups: 2 (over y), feat: 4 (over z), dp: 4 (over x, core).
Axes of the slice: x: 2, y: 2, z: 4, core: 2. Of those that a mesh axis runs over, the one named last changes fastest.
Arguments:
- features: bfloat16 [2048, 8192], P(('groups', 'dp'), 'feat'), parts along dimension 0, may hold values from -6 to 6
- bn_gain: float32 [8192], P('feat'), may hold values from 0.1 to 1.9
- bn_shift: float32 [8192], P('feat'), may hold values from -0.5 to 0.5
- weight: bfloat16 [8192, 8192], P('feat'), may hold values from -2 to 2
Outputs:
- covariance: float32 [16384, 8192], P(('groups', 'dp'), 'feat'), parts along dimension 0
- grad_in: bfloat16 [2048, 8192], P(('groups', 'dp'), 'feat'), parts along dimension 0
There are 2 independent parts, one for each index of `groups`. A program takes and returns all parts, laid end to end along the dimension named above; an argument that names none is the same for every part. Nothing has to cross between parts.
All inputs are finite; a program needn't handle non-finite values.
Results may differ from a plain program's by a relative error of at most 0.014.
Values may be sent and summed in bfloat16 or wider, within the bound.
A program may use at most 256 MiB of HBM per device.

v0:
```python
import jax
import jax.numpy as jnp
from jax import lax
from jax.sharding import PartitionSpec as P


def swap(value, distance):
    count = lax.axis_size("dp")
    return lax.ppermute(value, "dp", [(i, i ^ distance) for i in range(count)])


def block_order(count):
    order = [0]
    bit = count // 2
    while bit:
        order = order + [o ^ bit for o in order]
        bit //= 2
    return order


def gather_rows(value):
    bit = lax.axis_size("dp") // 2
    while bit:
        value = jnp.concatenate([value, swap(value, bit)], 0)
        bit //= 2
    return value


def column_blocks(full):
    count = lax.axis_size("dp")
    width = full.shape[1] // count
    me = lax.axis_index("dp")
    return [lax.dynamic_slice_in_dim(full, (me ^ o) * width, width, 1) for o in block_order(count)]


def exchange(blocks):
    order = block_order(lax.axis_size("dp"))
    return jnp.concatenate([swap(b, o) if o else b for b, o in zip(blocks, order)], 0)


def shards(features, bn_gain, bn_shift, weight):
    dp_count = lax.axis_size("dp")
    feat_count = lax.axis_size("feat")
    local_rows = features.shape[0]
    images = local_rows * dp_count
    hidden = features.astype(jnp.float32)
    col_sums, col_squares = lax.psum((jnp.sum(hidden, 0), jnp.sum(hidden * hidden, 0)), "dp")
    mean_h = col_sums / images
    var_h = col_squares / images - mean_h * mean_h
    normed = (hidden - mean_h) * lax.rsqrt(var_h + 1e-05) * bn_gain + bn_shift
    activated = jnp.maximum(normed, 0.0).astype(jnp.bfloat16)
    partial_value = jnp.dot(activated, weight, preferred_element_type=jnp.float32).astype(
        jnp.bfloat16
    )
    proj_f = lax.psum_scatter(partial_value, "feat", scatter_dimension=1, tiled=True).astype(
        jnp.float32
    )
    proj_mean = lax.psum(jnp.sum(proj_f, 0), "dp") / images
    centered = (proj_f - proj_mean).astype(jnp.bfloat16)
    cent_full = lax.all_gather(centered, "feat", axis=1, tiled=True)
    piece = gather_rows(centered)
    gram = lax.dot_general(
        centered, piece, (((1,), (1,)), ((), ())), preferred_element_type=jnp.float32
    )
    piece_f = piece.astype(jnp.float32)
    proj_var = jnp.sum(piece_f * piece_f, 0) / (images - 1)
    spread = jnp.sqrt(proj_var + 0.0001)
    scale_up = images / (images - 1)
    active = jnp.where(spread < 1.0, 1.0 / spread, 0.0)
    factor = lax.all_gather(
        4.0 * scale_up * proj_var + 25.0 * scale_up * active, "feat", axis=0, tiled=True
    )
    cent_full, factor, _ = lax.optimization_barrier((cent_full, factor, gram))
    gram = lax.psum(gram, "feat")
    cent_full, cuts = lax.optimization_barrier((cent_full, column_blocks(cent_full)))
    cent_x = exchange(cuts)
    scaled = (cent_full.astype(jnp.float32) * factor).astype(jnp.bfloat16)
    dims = (((1,), (1,)), ((), ()))
    through = lax.dot_general(cent_full, weight, dims, preferred_element_type=jnp.float32)
    direct = lax.dot_general(scaled, weight, dims, preferred_element_type=jnp.float32)
    through_all = gather_rows(through.astype(jnp.bfloat16))
    covariance = lax.dot_general(
        cent_x, piece, (((0,), (0,)), ((), ())), preferred_element_type=jnp.float32
    ) / (images - 1)
    gram, covariance = lax.optimization_barrier((gram, covariance))
    own = jnp.arange(local_rows, dtype=jnp.int32)[:, None]
    same = own == jnp.arange(images, dtype=jnp.int32)[None, :]
    gram = gram * (4.0 * scale_up / (images - 1))
    diag = jnp.sum(jnp.where(same, gram, 0.0), 1, keepdims=True)
    rest = jnp.where(same, 0.0, gram).astype(jnp.bfloat16)
    grad_in = (
        jnp.dot(rest, through_all, preferred_element_type=jnp.float32) + diag * through - direct
    )
    return (covariance, grad_in.astype(jnp.bfloat16))


def solution(mesh):
    in_specs = (P(("groups", "dp"), "feat"), P("feat"), P("feat"), P("feat", None))
    out_specs = (P(("groups", "dp"), "feat"), P(("groups", "dp"), "feat"))
    return jax.shard_map(shards, mesh=mesh, in_specs=in_specs, out_specs=out_specs, check_vma=False)
```

profile of v0, /device:TPU:0, one launch (start us, length us, event | category | flops | bytes accessed | tf_op | source)
XLA Modules:
  0.0 327.4 jit_solution(5208170377373880028)
XLA Ops:
  7.2 1.5 convert_reduce_fusion
  8.7 12.7 %all-reduce = (f32[2048]{0:T(1024)S(1)}, f32[2048]{0:T(1024)S(1)}) all-reduce(f32[2048]{0:T(1024)S(1)} %get-tuple-element.21, f32[2048]{0:T(1024)S(1)} %get-tuple-element.20), channel_id=1, replica_groups=mesh['groups'=2,'feat'=4,'dp'=4] {'dp'}, use_global_device_ids=true, to_apply=%region_3.0 | all-reduce | flops 4096 | bytes 32768 | tf_op jit(solution)/shard_map/psum | solution.py:47
  21.4 16.7 %convolution_convert_fusion = bf16[256,8192]{1,0:T(8,128)(2,1)} fusion(bf16[2048,8192]{1,0:T(8,128)(2,1)} %param.7, bf16[256,2048]{1,0:T(8,128)(2,1)} %param.4, f32[2048]{0:T(1024)} %param.6, f32[2048]{0:T(1024)} %param.5, f32[2048]{0:T(1024)S(1)} %get-tuple-element.29, f32[2048]{0:T(1024)S(1)} %get-tuple-element.28), kind=kOutput, calls=%fused_computation | convolution fusion | flops 8595701760 | bytes 38830080 | tf_op jit(solution)/shard_map/dot_general | solution.py:52
  38.2 77.2 %reduce-scatter.2.cloned.1.call-done = bf16[256,2048]{1,0:T(8,128)(2,1)} async-done(((bf16[256,8192]{1,0:T(8,128)(2,1)}), bf16[256,2048]{1,0:T(8,128)(2,1)}) %reduce-scatter.2.cloned.1.call-update) | async-done | bytes 1048592 | tf_op jit(solution)/shard_map/reduce_scatter | solution.py:55
  115.4 1.4 convert_reduce_fusion.1
  116.8 7.0 %psum.30 = f32[2048]{0:T(1024)S(1)} all-reduce(f32[2048]{0:T(1024)S(1)} %convert_reduce_fusion.1), channel_id=1, replica_groups=mesh['groups'=2,'feat'=4,'dp'=4] {'dp'}, use_global_device_ids=true, to_apply=%region_6.0 | all-reduce | flops 2048 | bytes 16384 | tf_op jit(solution)/shard_map/psum | solution.py:58
  123.8 2.4 fusion.24
  126.9 23.4 %collective-permute-done = bf16[256,2048]{1,0:T(8,128)(2,1)S(1)} collective-permute-done((bf16[256,2048]{1,0:T(8,128)(2,1)}, bf16[256,2048]{1,0:T(8,128)(2,1)S(1)}, u32[]{:S(2)}, u32[]{:S(2)}) %collective-permute-start) | collective-permute-done | bytes 1048608 | tf_op jit(solution)/shard_map/ppermute | solution.py:9
  150.3 2.8 pad_maximum_fusion.1
  153.1 4.5 %collective-permute-done.1 = bf16[512,2048]{1,0:T(8,128)(2,1)} collective-permute-done((bf16[512,2048]{1,0:T(8,128)(2,1)}, bf16[512,2048]{1,0:T(8,128)(2,1)}, u32[]{:S(2)}, u32[]{:S(2)}) %collective-permute-start.1) | collective-permute-done | bytes 2097184 | tf_op jit(solution)/shard_map/ppermute | solution.py:9
  157.6 2.2 multiply_reduce_fusion
  159.8 15.5 %all_gather.7 = f32[8192]{0:T(1024)S(1)} all-gather(f32[2048]{0:T(1024)S(1)} %multiply_add_fusion), channel_id=1, replica_groups=mesh['groups'=2,'feat'=4,'dp'=4] {'feat'}, dimensions={0}, use_global_device_ids=true | all-gather | bytes 40960 | tf_op jit(solution)/shard_map/all_gather | solution.py:70
  175.3 3.9 %fusion.44 = f32[256,1024]{1,0:T(8,128)} fusion(bf16[256,2048]{1,0:T(8,128)(2,1)S(1)} %copy-done, bf16[512,2048]{1,0:T(8,128)(2,1)} %collective-permute-done.1, bf16[256,2048]{1,0:T(8,128)(2,1)S(1)} %collective-permute-done), kind=kOutput, calls=%fused_computation.61 | convolution fusion | flops 1086324736 | bytes 5242880 | tf_op jit(solution)/shard_map/dot_general | solution.py:62
  179.2 28.0 %all-gather.2.cloned.1.call-done = bf16[256,8192]{1,0:T(8,128)(2,1)} async-done(((bf16[256,2048]{1,0:T(8,128)(2,1)}), bf16[256,8192]{1,0:T(8,128)(2,1)}) %all-gather.2.cloned.1.call-update) | async-done | bytes 4194320 | tf_op jit(solution)/shard_map/all_gather | solution.py:60
  207.2 4.0 %constant_dynamic-slice_fusion = (bf16[256,2048]{1,0:T(8,128)(2,1)}, bf16[256,2048]{1,0:T(8,128)(2,1)}, bf16[256,2048]{1,0:T(8,128)(2,1)}, bf16[256,2048]{1,0:T(8,128)(2,1)S(1)}) fusion(bf16[256,8192]{1,0:T(8,128)(2,1)} %all-gather.2.cloned.1.call-done, s32[]{:T(128)S(6)} %select_n.28, s32[]{:T(128)S(6)} %select_n.27, s32[]{:T(128)S(6)} %select_n.26, ...), kind=kLoop, calls=%fused_computation.52 | loop fusion | bytes 8388624 | tf_op jit(solution)/shard_map/dynamic_slice | solution.py:33
  211.2 17.4 %fusion.45 = (bf16[256,2048]{1,0:T(8,128)(2,1)}, f32[256,2048]{1,0:T(8,128)}) fusion(bf16[256,8192]{1,0:T(8,128)(2,1)} %all-gather.2.cloned.1.call-done, bf16[2048,8192]{1,0:T(8,128)(2,1)} %param.7), kind=kOutput, calls=%fused_computation.62 | convolution fusion | flops 8590458880 | bytes 40894464 | tf_op jit(solution)/shard_map/dot_general | solution.py:79
  228.6 1.5 collective-permute-start.5
  230.8 1.5 collective-permute-start.2
  232.3 22.7 %collective-permute-done.5 = bf16[256,2048]{1,0:T(8,128)(2,1)} collective-permute-done((bf16[256,2048]{1,0:T(8,128)(2,1)}, bf16[256,2048]{1,0:T(8,128)(2,1)}, u32[]{:S(2)}, u32[]{:S(2)}) %collective-permute-start.5) | collective-permute-done | bytes 1048608 | tf_op jit(solution)/shard_map/ppermute | solution.py:9
  254.9 3.2 pad_maximum_fusion.2
  258.1 17.3 %fusion = f32[256,2048]{1,0:T(8,128)} fusion(bf16[2048,8192]{1,0:T(8,128)(2,1)} %param.7, bf16[256,8192]{1,0:T(8,128)(2,1)} %all-gather.2.cloned.1.call-done, f32[8192]{0:T(1024)S(1)} %all_gather.7), kind=kOutput, calls=%fused_computation.4 | convolution fusion | flops 8596226048 | bytes 39878656 | tf_op jit(solution)/shard_map/dot_general | solution.py:80
  276.4 22.3 %collective-permute-done.2 = bf16[256,2048]{1,0:T(8,128)(2,1)} collective-permute-done((bf16[256,2048]{1,0:T(8,128)(2,1)}, bf16[256,2048]{1,0:T(8,128)(2,1)}, u32[]{:S(2)}, u32[]{:S(2)}) %collective-permute-start.2) | collective-permute-done | bytes 1048608 | tf_op jit(solution)/shard_map/ppermute | solution.py:9
  298.7 14.7 %convolution_multiply_fusion = f32[2048,2048]{1,0:T(8,128)} fusion(bf16[256,2048]{1,0:T(8,128)(2,1)} %collective-permute-done.4, bf16[256,2048]{1,0:T(8,128)(2,1)} %collective-permute-done.3, bf16[256,2048]{1,0:T(8,128)(2,1)} %collective-permute-done.2, bf16[256,2048]{1,0:T(8,128)(2,1)S(1)} %get-tuple-element.12, ...), kind=kOutput, calls=%fused_computation.1 | convolution fusion | flops 8623489024 | bytes 25165824 | tf_op jit(solution)/shard_map/dot_general | solution.py:82
  314.8 6.1 %fusion.21 = bf16[256,2048]{1,0:T(8,128)(2,1)} fusion(f32[256,2048]{1,0:T(8,128)} %fusion, bf16[512,2048]{1,0:T(8,128)(2,1)} %collective-permute-done.6, bf16[256,2048]{1,0:T(8,128)(2,1)} %collective-permute-done.5, bf16[256,2048]{1,0:T(8,128)(2,1)} %get-tuple-element.30, f32[256,2048]{1,0:T(8,128)} %get-tuple-element.31, f32[256]{0:T(256)S(1)} %select_reduce_fusion, ...), kind=kOutput, calls=%fused_computation.27 | convolution fusion | flops 1089470464 | bytes 10486784 | tf_op jit(solution)/shard_map/dot_general | solution.py:92
  (21 shorter events, 3.9 us)
Async XLA Ops:
  7.2 108.3 %reduce-scatter.2.cloned.1.call-start = ((), (), s32[]{:S(2)}) async-start(), calls=%async_computation.1 | async-start | bytes 5242880 | tf_op jit(solution)/shard_map/reduce_scatter | solution.py:55
  38.2 169.0 %all-gather.2.cloned.1.call-start = ((), (), s32[]{:S(2)}) async-start(), calls=%async_computation.3 | async-start | bytes 5242880 | tf_op jit(solution)/shard_map/all_gather | solution.py:60
  126.3 31.4 %copy-start = (bf16[256,2048]{1,0:T(8,128)(2,1)S(1)}, bf16[256,2048]{1,0:T(8,128)(2,1)}, u32[]{:S(2)}) copy-start(bf16[256,2048]{1,0:T(8,128)(2,1)} %fusion.24) | copy-start | bytes 3145732
  126.3 187.1 %all-reduce.3.cloned.1.call-start = ((), (), s32[]{:S(2)}) async-start(), calls=%async_computation.2 | async-start | bytes 2097152 | tf_op jit(solution)/shard_map/psum | solution.py:74
  126.3 24.0 %collective-permute-start = (bf16[256,2048]{1,0:T(8,128)(2,1)}, bf16[256,2048]{1,0:T(8,128)(2,1)S(1)}, u32[]{:S(2)}, u32[]{:S(2)}) collective-permute-start(bf16[256,2048]{1,0:T(8,128)(2,1)} %fusion.24), channel_id=1, source_target_pairs={{0,2},{1,3},{2,0},{3,1},{4,6},{5,7},{6,4},{7,5},{8,10},{9,11},{10,... | collective-permute-start | bytes 3145736 | tf_op jit(solution)/shard_map/ppermute | solution.py:9
  153.1 4.5 %collective-permute-start.1 = (bf16[512,2048]{1,0:T(8,128)(2,1)}, bf16[512,2048]{1,0:T(8,128)(2,1)}, u32[]{:S(2)}, u32[]{:S(2)}) collective-permute-start(bf16[512,2048]{1,0:T(8,128)(2,1)} %pad_maximum_fusion.1), channel_id=1, source_target_pairs={{0,1},{1,0},{2,3},{3,2},{4,5},{5,4},{6,7},{7,6},{8,9},{9,8},{10,11... | collective-permute-start | bytes 6291464 | tf_op jit(solution)/shard_map/ppermute | solution.py:9
  228.6 26.4 %collective-permute-start.5 = (bf16[256,2048]{1,0:T(8,128)(2,1)}, bf16[256,2048]{1,0:T(8,128)(2,1)}, u32[]{:S(2)}, u32[]{:S(2)}) collective-permute-start(bf16[256,2048]{1,0:T(8,128)(2,1)} %get-tuple-element.30), channel_id=1, source_target_pairs={{0,2},{1,3},{2,0},{3,1},{4,6},{5,7},{6,4},{7,5},{8,10},{9,11},{10,... | collective-permute-start | bytes 3145736 | tf_op jit(solution)/shard_map/ppermute | solution.py:9
  230.1 46.3 %collective-permute-start.4 = (bf16[256,2048]{1,0:T(8,128)(2,1)}, bf16[256,2048]{1,0:T(8,128)(2,1)}, u32[]{:S(2)}, u32[]{:S(2)}) collective-permute-start(bf16[256,2048]{1,0:T(8,128)(2,1)} %get-tuple-element.15), channel_id=1, source_target_pairs={{0,3},{1,2},{2,1},{3,0},{4,7},{5,6},{6,5},{7,4},{8,11},{9,10},{10,... | collective-permute-start | bytes 3145736 | tf_op jit(solution)/shard_map/ppermute | solution.py:9
  230.1 46.3 %collective-permute-start.3 = (bf16[256,2048]{1,0:T(8,128)(2,1)}, bf16[256,2048]{1,0:T(8,128)(2,1)}, u32[]{:S(2)}, u32[]{:S(2)}) collective-permute-start(bf16[256,2048]{1,0:T(8,128)(2,1)} %get-tuple-element.14), channel_id=1, source_target_pairs={{0,1},{1,0},{2,3},{3,2},{4,5},{5,4},{6,7},{7,6},{8,9},{9,8},{10,11... | collective-permute-start | bytes 3145736 | tf_op jit(solution)/shard_map/ppermute | solution.py:9
  230.8 67.9 %collective-permute-start.2 = (bf16[256,2048]{1,0:T(8,128)(2,1)}, bf16[256,2048]{1,0:T(8,128)(2,1)}, u32[]{:S(2)}, u32[]{:S(2)}) collective-permute-start(bf16[256,2048]{1,0:T(8,128)(2,1)} %get-tuple-element.13), channel_id=1, source_target_pairs={{0,2},{1,3},{2,0},{3,1},{4,6},{5,7},{6,4},{7,5},{8,10},{9,11},{10,... | collective-permute-start | bytes 3145736 | tf_op jit(solution)/shard_map/ppermute | solution.py:9
  258.1 56.7 %collective-permute-start.6 = (bf16[512,2048]{1,0:T(8,128)(2,1)}, bf16[512,2048]{1,0:T(8,128)(2,1)}, u32[]{:S(2)}, u32[]{:S(2)}) collective-permute-start(bf16[512,2048]{1,0:T(8,128)(2,1)} %pad_maximum_fusion.2), channel_id=1, source_target_pairs={{0,1},{1,0},{2,3},{3,2},{4,5},{5,4},{6,7},{7,6},{8,9},{9,8},{10,11... | collective-permute-start | bytes 6291464 | tf_op jit(solution)/shard_map/ppermute | solution.py:9
Sparse Core Ops, SparseCore 0:
  38.3 77.0 reduce-scatter.1
  126.4 80.7 all-gather.1
  230.2 49.4 all-reduce.2
where the time goes:
time: 328 us; the launch traced here: 327 us
  waiting for transfers between devices  179 us (55%)
  matrix products  76.1 us (23%)
  blocking collectives  35.1 us (11%)
  other arithmetic  14.9 us (5%)
  between operations  13.8 us (4%)
  starting transfers between devices  4.41 us (1%)
  local copies, waits for them, and re-layouts  3.97 us (1%)
    reduce_scatter x1, waiting for transfers between devices, shards(): lax.psum_scatter(partial_value, 'feat', scatter_dimension=1, tiled=True)  77.2 us
    ppermute x7, waiting for transfers between devices, swap(): return lax.ppermute(value, 'dp', [(i, i ^ distance) for i in range(count)])  73.9 us
    all_gather x1, waiting for transfers between devices, shards(): cent_full = lax.all_gather(centered, 'feat', axis=1, tiled=True)  28 us
    dot_general x1, matrix products, shards(): lax.dot_general(cent_full, weight, dims, preferred_element_type=jnp.float32)  17.4 us
    dot_general x1, matrix products, shards(): lax.dot_general(scaled, weight, dims, preferred_element_type=jnp.float32)  17.3 us
    dot_general x1, matrix products, shards(): jnp.dot(activated, weight, preferred_element_type=jnp.float32)  16.7 us
    all_gather x1, blocking collectives, shards(): lax.all_gather(4.0 * scale_up * proj_var + 25.0 * scale_up * active, 'fea...  15.5 us
    dot_general x1, matrix products, shards(): lax.dot_general(cent_x, piece, (((0,), (0,)), ((), ())), preferred_elemen...  14.7 us
  transfers between devices with their start and end apart: 10, of which 7 were waited for; matrix products, arithmetic and copies ran while one was open for 14% of the time, Pallas kernels for 0%

commit v1 on v0

--- a/solution.py
+++ b/solution.py
@@ -57,7 +57,14 @@
     )
     proj_mean = lax.psum(jnp.sum(proj_f, 0), "dp") / images
     centered = (proj_f - proj_mean).astype(jnp.bfloat16)
-    cent_full = lax.all_gather(centered, "feat", axis=1, tiled=True)
+    count_2 = lax.axis_size("feat")
+    route = [(i_2, (i_2 + 1) % count_2) for i_2 in range(count_2)]
+    pieces = [centered]
+    for far in range(1, count_2):
+        pieces = [lax.ppermute(pieces[0], "feat", route), *pieces]
+    whole = jnp.concatenate(pieces, axis=1)
+    places = (lax.axis_index("feat") + 1) * pieces[-1].shape[1]
+    cent_full = jnp.roll(whole, places, axis=1)
     piece = gather_rows(centered)
     gram = lax.dot_general(
         centered, piece, (((1,), (1,)), ((), ())), preferred_element_type=jnp.float32

time: 328 us -> 340 us (1.037)
  waiting for transfers between devices: 179 us -> 187 us
  local copies, waits for them, and re-layouts: 3.97 us -> 10.6 us
  starting transfers between devices: 4.41 us -> 8.68 us
  other arithmetic: 14.9 us -> 11.5 us
    ppermute x0 -> x3, waiting for transfers between devices: none -> 69.5 us  [shards(): pieces = [lax.ppermute(pieces[0], 'feat', route), *pieces]]
    ppermute x7, waiting for transfers between devices: 73.9 us -> 40.1 us  [swap(): return lax.ppermute(value, 'dp', [(i, i ^ distance) for i in range(count)])]
    all_gather x1 -> x0, waiting for transfers between devices: 28 us -> none  [shards(): cent_full = lax.all_gather(centered, 'feat', axis=1, tiled=True)]
    unnamed x2 -> x16, local copies, waits for them, and re-layouts: 0.01 us -> 3.86 us
  transfers between devices with their start and end apart: 10 -> 12, of which waited for: 7 -> 7; matrix products, arithmetic and copies ran while one was open for 14% -> 12% of each run, Pallas kernels for 0% -> 0%
where the time goes in v1:
time: 340 us
  waiting for transfers between devices  187 us (55%)
  matrix products  75.2 us (22%)
  blocking collectives  32.8 us (10%)
  between operations  14.2 us (4%)
  other arithmetic  11.5 us (3%)
  local copies, waits for them, and re-layouts  10.6 us (3%)
  starting transfers between devices  8.68 us (3%)
    reduce_scatter x1, waiting for transfers between devices, shards(): lax.psum_scatter(partial_value, 'feat', scatter_dimension=1, tiled=True)  77.2 us
    ppermute x3, waiting for transfers between devices, shards(): pieces = [lax.ppermute(pieces[0], 'feat', route), *pieces]  69.5 us
    ppermute x7, waiting for transfers between devices, swap(): return lax.ppermute(value, 'dp', [(i, i ^ distance) for i in range(count)])  40.1 us
    dot_general x1, matrix products, shards(): lax.dot_general(scaled, weight, dims, preferred_element_type=jnp.float32)  17.4 us
    dot_general x1, matrix products, shards(): lax.dot_general(cent_full, weight, dims, preferred_element_type=jnp.float32)  17 us
    dot_general x1, matrix products, shards(): jnp.dot(activated, weight, preferred_element_type=jnp.float32)  16.7 us
    dot_general x1, matrix products, shards(): lax.dot_general(cent_x, piece, (((0,), (0,)), ((), ())), preferred_elemen...  14.5 us
    all_gather x1, blocking collectives, shards(): lax.all_gather(4.0 * scale_up * proj_var + 25.0 * scale_up * active, 'fea...  13.1 us
  transfers between devices with their start and end apart: 12, of which 7 were waited for; matrix products, arithmetic and copies ran while one was open for 12% of the time, Pallas kernels for 0%

profile of v1, /device:TPU:0, one launch (start us, length us, event | category | flops | bytes accessed | tf_op | source)
XLA Modules:
  0.0 339.8 jit_solution(2377157389512464793)
XLA Ops:
  7.2 1.5 convert_reduce_fusion
  8.7 12.7 %all-reduce = (f32[2048]{0:T(1024)S(1)}, f32[2048]{0:T(1024)S(1)}) all-reduce(f32[2048]{0:T(1024)S(1)} %get-tuple-element.21, f32[2048]{0:T(1024)S(1)} %get-tuple-element.20), channel_id=1, replica_groups=mesh['groups'=2,'feat'=4,'dp'=4] {'dp'}, use_global_device_ids=true, to_apply=%region_3.0 | all-reduce | flops 4096 | bytes 32768 | tf_op jit(solution)/shard_map/psum | solution.py:47
  21.4 16.7 %convolution_convert_fusion = bf16[256,8192]{1,0:T(8,128)(2,1)} fusion(bf16[2048,8192]{1,0:T(8,128)(2,1)} %param.7, bf16[256,2048]{1,0:T(8,128)(2,1)} %param.4, f32[2048]{0:T(1024)} %param.6, f32[2048]{0:T(1024)} %param.5, f32[2048]{0:T(1024)S(1)} %get-tuple-element.29, f32[2048]{0:T(1024)S(1)} %get-tuple-element.28), kind=kOutput, calls=%fused_computation | convolution fusion | flops 8595701760 | bytes 38830080 | tf_op jit(solution)/shard_map/dot_general | solution.py:52
  38.2 77.2 %reduce-scatter.2.cloned.1.call-done = bf16[256,2048]{1,0:T(8,128)(2,1)} async-done(((bf16[256,8192]{1,0:T(8,128)(2,1)}), bf16[256,2048]{1,0:T(8,128)(2,1)}) %reduce-scatter.2.cloned.1.call-update) | async-done | bytes 1048592 | tf_op jit(solution)/shard_map/reduce_scatter | solution.py:55
  116.8 7.0 %psum.30 = f32[2048]{0:T(1024)S(1)} all-reduce(f32[2048]{0:T(1024)S(1)} %convert_reduce_fusion.1), channel_id=1, replica_groups=mesh['groups'=2,'feat'=4,'dp'=4] {'dp'}, use_global_device_ids=true, to_apply=%region_6.0 | all-reduce | flops 2048 | bytes 16384 | tf_op jit(solution)/shard_map/psum | solution.py:58
  125.3 1.5 collective-permute-start.2
  126.8 24.1 %collective-permute-done.2 = bf16[256,2048]{1,0:T(8,128)(2,1)S(1)} collective-permute-done((bf16[256,2048]{1,0:T(8,128)(2,1)S(1)}, bf16[256,2048]{1,0:T(8,128)(2,1)S(1)}, u32[]{:S(2)}, u32[]{:S(2)}) %collective-permute-start.2) | collective-permute-done | bytes 1048608 | tf_op jit(solution)/shard_map/ppermute | solution.py:64
  152.3 23.1 %collective-permute-done.3 = bf16[256,2048]{1,0:T(8,128)(2,1)S(1)} collective-permute-done((bf16[256,2048]{1,0:T(8,128)(2,1)S(1)}, bf16[256,2048]{1,0:T(8,128)(2,1)S(1)}, u32[]{:S(2)}, u32[]{:S(2)}) %collective-permute-start.3) | collective-permute-done | bytes 1048608 | tf_op jit(solution)/shard_map/ppermute | solution.py:64
  176.9 22.3 %collective-permute-done.4 = bf16[256,2048]{1,0:T(8,128)(2,1)} collective-permute-done((bf16[256,2048]{1,0:T(8,128)(2,1)S(1)}, bf16[256,2048]{1,0:T(8,128)(2,1)}, u32[]{:S(2)}, u32[]{:S(2)}) %collective-permute-start.4) | collective-permute-done | bytes 1048608 | tf_op jit(solution)/shard_map/ppermute | solution.py:64
  202.6 2.3 constant_dynamic-slice_fusion.4
  204.9 2.4 multiply_reduce_fusion
  207.3 13.1 %all_gather.3 = f32[8192]{0:T(1024)S(1)} all-gather(f32[2048]{0:T(1024)S(1)} %multiply_add_fusion), channel_id=1, replica_groups=mesh['groups'=2,'feat'=4,'dp'=4] {'feat'}, dimensions={0}, use_global_device_ids=true | all-gather | bytes 40960 | tf_op jit(solution)/shard_map/all_gather | solution.py:77
  220.5 3.5 %fusion.44 = f32[256,1024]{1,0:T(8,128)} fusion(bf16[256,2048]{1,0:T(8,128)(2,1)S(1)} %fusion.24, bf16[512,2048]{1,0:T(8,128)(2,1)S(1)} %collective-permute-done.1, bf16[256,2048]{1,0:T(8,128)(2,1)} %collective-permute-done), kind=kOutput, calls=%fused_computation.70 | convolution fusion | flops 1086324736 | bytes 5242880 | tf_op jit(solution)/shard_map/dot_general | solution.py:69
  224.0 4.4 %constant_dynamic-slice_fusion = (bf16[256,2048]{1,0:T(8,128)(2,1)}, bf16[256,2048]{1,0:T(8,128)(2,1)}, bf16[256,2048]{1,0:T(8,128)(2,1)}, bf16[256,2048]{1,0:T(8,128)(2,1)}) fusion(bf16[256,8192]{1,0:T(8,128)(2,1)} %constant_dynamic-slice_fusion.4, s32[]{:T(128)S(6)} %select_n.43, s32[]{:T(128)S(6)} %select_n.42, s32[]{:T(128)S(6)} %select_n.41, ...), kind=kLoop, calls=%fused_computation.60 | loop fusion | bytes 8388624 | tf_op jit(solution)/shard_map/dynamic_slice | solution.py:33
  228.3 17.0 %fusion.45 = (bf16[256,2048]{1,0:T(8,128)(2,1)S(1)}, f32[256,2048]{1,0:T(8,128)}) fusion(bf16[256,8192]{1,0:T(8,128)(2,1)} %constant_dynamic-slice_fusion.4, bf16[2048,8192]{1,0:T(8,128)(2,1)} %param.7), kind=kOutput, calls=%fused_computation.71 | convolution fusion | flops 8590458880 | bytes 40894464 | tf_op jit(solution)/shard_map/dot_general | solution.py:86
  245.4 3.3 collective-permute-start.8
  248.9 2.0 collective-permute-start.5
  251.0 21.8 %collective-permute-done.8 = bf16[256,2048]{1,0:T(8,128)(2,1)S(1)} collective-permute-done((bf16[256,2048]{1,0:T(8,128)(2,1)S(1)}, bf16[256,2048]{1,0:T(8,128)(2,1)S(1)}, u32[]{:S(2)}, u32[]{:S(2)}) %collective-permute-start.8) | collective-permute-done | bytes 1048608 | tf_op jit(solution)/shard_map/ppermute | solution.py:9
  273.8 1.5 pad_maximum_fusion.2
  275.3 17.4 %fusion = f32[256,2048]{1,0:T(8,128)} fusion(bf16[2048,8192]{1,0:T(8,128)(2,1)} %param.7, bf16[256,8192]{1,0:T(8,128)(2,1)} %constant_dynamic-slice_fusion.4, f32[8192]{0:T(1024)S(1)} %all_gather.3), kind=kOutput, calls=%fused_computation.4 | convolution fusion | flops 8596226048 | bytes 39878656 | tf_op jit(solution)/shard_map/dot_general | solution.py:87
  292.7 2.2 collective-permute-done.7
  294.9 16.1 %collective-permute-done.5 = bf16[256,2048]{1,0:T(8,128)(2,1)} collective-permute-done((bf16[256,2048]{1,0:T(8,128)(2,1)}, bf16[256,2048]{1,0:T(8,128)(2,1)}, u32[]{:S(2)}, u32[]{:S(2)}) %collective-permute-start.5) | collective-permute-done | bytes 1048608 | tf_op jit(solution)/shard_map/ppermute | solution.py:9
  311.0 14.5 %convolution_multiply_fusion = f32[2048,2048]{1,0:T(8,128)} fusion(bf16[256,2048]{1,0:T(8,128)(2,1)} %collective-permute-done.7, bf16[256,2048]{1,0:T(8,128)(2,1)} %collective-permute-done.6, bf16[256,2048]{1,0:T(8,128)(2,1)} %collective-permute-done.5, bf16[256,2048]{1,0:T(8,128)(2,1)} %get-tuple-element.12, bf16[512,2048]{1,0:T(8,128)(2,1)S(1)} %copy-done.2, ...), kind=kOutput, calls=%fused_computation.1 | convolution fusion | flops 8623489024 | bytes 25165824 | tf_op jit(solution)/shard_map/dot_general | solution.py:89
  326.8 6.1 %fusion.21 = bf16[256,2048]{1,0:T(8,128)(2,1)} fusion(f32[256,2048]{1,0:T(8,128)} %fusion, bf16[512,2048]{1,0:T(8,128)(2,1)} %collective-permute-done.9, bf16[256,2048]{1,0:T(8,128)(2,1)} %copy-done.4, bf16[256,2048]{1,0:T(8,128)(2,1)} %copy-done.3, f32[256,2048]{1,0:T(8,128)} %get-tuple-element.31, f32[256]{0:T(256)S(1)} %select_reduce_fusion, ...), kind=kOutput, calls=%fused_computation.27 | convolution fusion | flops 1089470464 | bytes 10486784 | tf_op jit(solution)/shard_map/dot_general | solution.py:99
  (41 shorter events, 11.7 us)
Async XLA Ops:
  7.2 108.3 %reduce-scatter.2.cloned.1.call-start = ((), (), s32[]{:S(2)}) async-start(), calls=%async_computation.1 | async-start | bytes 5242880 | tf_op jit(solution)/shard_map/reduce_scatter | solution.py:55
  38.2 287.3 %all-reduce.3.cloned.1.call-start = ((), (), s32[]{:S(2)}) async-start(), calls=%async_computation.2 | async-start | bytes 2097152 | tf_op jit(solution)/shard_map/psum | solution.py:81
  125.3 25.6 %collective-permute-start.2 = (bf16[256,2048]{1,0:T(8,128)(2,1)S(1)}, bf16[256,2048]{1,0:T(8,128)(2,1)S(1)}, u32[]{:S(2)}, u32[]{:S(2)}) collective-permute-start(bf16[256,2048]{1,0:T(8,128)(2,1)S(1)} %fusion.24), channel_id=1, source_target_pairs={{0,4},{4,8},{8,12},{12,0},{1,5},{5,9},{9,13},{13,1},{2,6},{6,10},{... | collective-permute-start | bytes 3145736 | tf_op jit(solution)/shard_map/ppermute | solution.py:64
  150.8 24.6 %collective-permute-start.3 = (bf16[256,2048]{1,0:T(8,128)(2,1)S(1)}, bf16[256,2048]{1,0:T(8,128)(2,1)S(1)}, u32[]{:S(2)}, u32[]{:S(2)}) collective-permute-start(bf16[256,2048]{1,0:T(8,128)(2,1)S(1)} %collective-permute-done.2), channel_id=1, source_target_pairs={{0,4},{4,8},{8,12},{12,0},{1,5},{5,9},{9,13},{13,1},{2,6},{6,10},{... | collective-permute-start | bytes 3145736 | tf_op jit(solution)/shard_map/ppermute | solution.py:64
  150.8 24.6 %collective-permute-start = (bf16[256,2048]{1,0:T(8,128)(2,1)S(1)}, bf16[256,2048]{1,0:T(8,128)(2,1)}, u32[]{:S(2)}, u32[]{:S(2)}) collective-permute-start(bf16[256,2048]{1,0:T(8,128)(2,1)S(1)} %fusion.24), channel_id=1, source_target_pairs={{0,2},{1,3},{2,0},{3,1},{4,6},{5,7},{6,4},{7,5},{8,10},{9,11},{10,... | collective-permute-start | bytes 3145736 | tf_op jit(solution)/shard_map/ppermute | solution.py:9
  175.4 23.8 %collective-permute-start.4 = (bf16[256,2048]{1,0:T(8,128)(2,1)S(1)}, bf16[256,2048]{1,0:T(8,128)(2,1)}, u32[]{:S(2)}, u32[]{:S(2)}) collective-permute-start(bf16[256,2048]{1,0:T(8,128)(2,1)S(1)} %collective-permute-done.3), channel_id=1, source_target_pairs={{0,4},{4,8},{8,12},{12,0},{1,5},{5,9},{9,13},{13,1},{2,6},{6,10},{... | collective-permute-start | bytes 3145736 | tf_op jit(solution)/shard_map/ppermute | solution.py:64
  176.8 23.8 %copy-start = (bf16[256,2048]{1,0:T(8,128)(2,1)S(1)}, bf16[256,2048]{1,0:T(8,128)(2,1)}, u32[]{:S(2)}) copy-start(bf16[256,2048]{1,0:T(8,128)(2,1)} %reduce-scatter.2.cloned.1.call-done) | copy-start | bytes 3145732
  176.8 28.1 %collective-permute-start.1 = (bf16[512,2048]{1,0:T(8,128)(2,1)S(1)}, bf16[512,2048]{1,0:T(8,128)(2,1)S(1)}, u32[]{:S(2)}, u32[]{:S(2)}) collective-permute-start(bf16[512,2048]{1,0:T(8,128)(2,1)S(1)} %pad_maximum_fusion.1), channel_id=1, source_target_pairs={{0,1},{1,0},{2,3},{3,2},{4,5},{5,4},{6,7},{7,6},{8,9},{9,8},{10,11... | collective-permute-start | bytes 6291464 | tf_op jit(solution)/shard_map/ppermute | solution.py:9
  204.9 15.6 %copy-start.1 = (bf16[512,2048]{1,0:T(8,128)(2,1)}, bf16[512,2048]{1,0:T(8,128)(2,1)S(1)}, u32[]{:S(2)}) copy-start(bf16[512,2048]{1,0:T(8,128)(2,1)S(1)} %collective-permute-done.1) | copy-start | bytes 6291460
  245.4 27.4 %copy-start.3 = (bf16[256,2048]{1,0:T(8,128)(2,1)}, bf16[256,2048]{1,0:T(8,128)(2,1)S(1)}, u32[]{:S(2)}) copy-start(bf16[256,2048]{1,0:T(8,128)(2,1)S(1)} %get-tuple-element.30) | copy-start | bytes 3145732
  245.4 27.4 %collective-permute-start.8 = (bf16[256,2048]{1,0:T(8,128)(2,1)S(1)}, bf16[256,2048]{1,0:T(8,128)(2,1)S(1)}, u32[]{:S(2)}, u32[]{:S(2)}) collective-permute-start(bf16[256,2048]{1,0:T(8,128)(2,1)S(1)} %get-tuple-element.30), channel_id=1, source_target_pairs={{0,2},{1,3},{2,0},{3,1},{4,6},{5,7},{6,4},{7,5},{8,10},{9,11},{10,... | collective-permute-start | bytes 3145736 | tf_op jit(solution)/shard_map/ppermute | solution.py:9
  248.7 46.2 %collective-permute-start.7 = (bf16[256,2048]{1,0:T(8,128)(2,1)}, bf16[256,2048]{1,0:T(8,128)(2,1)}, u32[]{:S(2)}, u32[]{:S(2)}) collective-permute-start(bf16[256,2048]{1,0:T(8,128)(2,1)} %get-tuple-element.15), channel_id=1, source_target_pairs={{0,3},{1,2},{2,1},{3,0},{4,7},{5,6},{6,5},{7,4},{8,11},{9,10},{10,... | collective-permute-start | bytes 3145736 | tf_op jit(solution)/shard_map/ppermute | solution.py:9
  248.8 46.1 %collective-permute-start.6 = (bf16[256,2048]{1,0:T(8,128)(2,1)}, bf16[256,2048]{1,0:T(8,128)(2,1)}, u32[]{:S(2)}, u32[]{:S(2)}) collective-permute-start(bf16[256,2048]{1,0:T(8,128)(2,1)} %get-tuple-element.14), channel_id=1, source_target_pairs={{0,1},{1,0},{2,3},{3,2},{4,5},{5,4},{6,7},{7,6},{8,9},{9,8},{10,11... | collective-permute-start | bytes 3145736 | tf_op jit(solution)/shard_map/ppermute | solution.py:9
  248.9 62.1 %collective-permute-start.5 = (bf16[256,2048]{1,0:T(8,128)(2,1)}, bf16[256,2048]{1,0:T(8,128)(2,1)}, u32[]{:S(2)}, u32[]{:S(2)}) collective-permute-start(bf16[256,2048]{1,0:T(8,128)(2,1)} %get-tuple-element.13), channel_id=1, source_target_pairs={{0,2},{1,3},{2,0},{3,1},{4,6},{5,7},{6,4},{7,5},{8,10},{9,11},{10,... | collective-permute-start | bytes 3145736 | tf_op jit(solution)/shard_map/ppermute | solution.py:9
  272.8 1.0 copy-start.4
  275.3 35.7 %copy-start.2 = (bf16[512,2048]{1,0:T(8,128)(2,1)S(1)}, bf16[512,2048]{1,0:T(8,128)(2,1)}, u32[]{:S(2)}) copy-start(bf16[512,2048]{1,0:T(8,128)(2,1)} %copy-done.1) | copy-start | bytes 6291460
  275.3 51.5 %collective-permute-start.9 = (bf16[512,2048]{1,0:T(8,128)(2,1)}, bf16[512,2048]{1,0:T(8,128)(2,1)}, u32[]{:S(2)}, u32[]{:S(2)}) collective-permute-start(bf16[512,2048]{1,0:T(8,128)(2,1)} %pad_maximum_fusion.2), channel_id=1, source_target_pairs={{0,1},{1,0},{2,3},{3,2},{4,5},{5,4},{6,7},{7,6},{8,9},{9,8},{10,11... | collective-permute-start | bytes 6291464 | tf_op jit(solution)/shard_map/ppermute | solution.py:9
Sparse Core Ops, SparseCore 0:
  38.3 77.0 reduce-scatter.1
  248.9 49.0 all-reduce.2
